TPU v7x, 512 devices: a whole 4x8x8 slice. The times are simulated.
512 devices in a mesh: lon: 32 (over x_lo, y, core), lat: 16 (over z, x_hi).
Axes of the slice: x: 4 (x_hi: 2, x_lo: 2; x = x_hi * 2 + x_lo), y: 8, z: 8, core: 2. Of those that a mesh axis runs over, the one named last changes fastest.
Arguments:
- potential_warmth: float32 [25, 256, 4096], P(None, 'lat', 'lon'), may hold values from -4 to 4
- saltiness_anomaly: float32 [25, 256, 4096], P(None, 'lat', 'lon'), may hold values from -4 to 4
- east_speed_array: float32 [25, 256, 4096], P(None, 'lat', 'lon'), may hold values from -1 to 1
- north_speed_array: float32 [25, 256, 4096], P(None, 'lat', 'lon'), may hold values from -1 to 1
- water_indicator: int32 [25, 256, 4096], P(None, 'lat', 'lon'), may hold values from 0 to 1, as said below
- bottom_layer_index: int32 [256, 4096], P('lat', 'lon'), may hold values from 0 to 25, as said below
Outputs:
- temperature_next: float32 [25, 256, 4096], P(None, 'lat', 'lon')
- salinity_next: float32 [25, 256, 4096], P(None, 'lat', 'lon')
- zonal_next: float32 [25, 256, 4096], P(None, 'lat', 'lon')
- meridional_next: float32 [25, 256, 4096], P(None, 'lat', 'lon')
Inputs may be any that keep to these rules, and one draw needn't show every extreme that they name: `bottom_layer_index`: 0 marks a land column; a sea column has this many wet levels. `water_indicator`: 1 exactly at the levels k of a column with k < bottom_layer_index of that column.
All inputs are finite; a program needn't handle non-finite values.
Results may differ from a plain program's by a relative error of at most 0.00016.
Values sent between devices are 32-bit elements; how exact they have to be, the bound alone decides.
A program may use at most 64 MiB of HBM per device.

v0:
```python
import functools

import jax
import jax.numpy as jnp
from jax import lax
from jax.experimental import pallas as pl
from jax.experimental.pallas import tpu as pltpu
from jax.sharding import PartitionSpec as P

SWEEPS = 4

courant = 0.3
mixing = 0.08
vertical_mixing = 0.1
buoyancy = 0.05
rotation = 0.2
drag_rate = 0.3
thermal = 0.25
haline = 0.2
cabbeling = 0.03

K = 25
R = 16
G = 4
LIN = (R + 2 * G) * K + 16
BLOCK = 56
HEAD = 8
CHUNKS = ((0, 112), (112, 96), (208, 104), (312, 96))
MSG = 408
PACKED = 104
CORNER = 32
KB = (0, 8, 16, 17)
N_MASK = 8

LON, LAT = "lon", "lat"


def lane(shape):
    return lax.broadcasted_iota(jnp.int32, shape, 1)


def density(t, s):
    h = 0.5 * buoyancy
    return t * (-thermal * h - (cabbeling * h) * t) + (haline * h) * s


def kernel(
    n_lon, n_lat, t_hbm, s_hbm, u_hbm, v_hbm, b_hbm, out_hbm,
    xin, bin_, m_st, q_st, m4, pm, pq, mk, qk, cor, bm, bq,
    pack, pack_w, pack_e, send_n, send_s, recv_n, recv_s, csend_n, csend_s, crecv_n, crecv_s,
    in_sem, out_sem, lon_ss, lon_rs, n_ss, n_rs, s_ss, s_rs,
):
    i = lax.axis_index(LON)
    j = lax.axis_index(LAT)
    top = j == n_lat - 1
    east = lax.rem(i + 1, n_lon)
    west = lax.rem(i + n_lon - 1, n_lon)
    has_south = j > 0
    north = {LON: jnp.where(top, n_lon - 1 - i, i), LAT: jnp.where(top, j, j + 1)}
    south = {LON: i, LAT: jnp.maximum(j - 1, 0)}
    mesh_id = pl.DeviceIdType.MESH

    barrier = pltpu.get_barrier_semaphore()
    pl.semaphore_signal(barrier, inc=1, device_id={LON: east, LAT: j}, device_id_type=mesh_id)
    pl.semaphore_signal(barrier, inc=1, device_id={LON: west, LAT: j}, device_id_type=mesh_id)
    pl.semaphore_signal(barrier, inc=1, device_id=north, device_id_type=mesh_id)

    @pl.when(has_south)
    def _():
        pl.semaphore_signal(barrier, inc=1, device_id=south, device_id_type=mesh_id)

    loads = [
        pltpu.make_async_copy(ref, xin.at[f], in_sem.at[f])
        for f, ref in enumerate((t_hbm, s_hbm, u_hbm, v_hbm))
    ]
    loads.append(pltpu.make_async_copy(b_hbm, bin_, in_sem.at[4]))
    for c in loads:
        c.start()
    for c in loads:
        c.wait()

    lanes8 = lane((8, 128))
    group8 = lanes8 // 8

    bm[pl.ds(G, R), :] = bin_[...].astype(jnp.float32)
    tiles = [(f, k, h) for f in range(4) for k in range(K) for h in range(2)]
    tiles += [(4, 0, 0), (4, 0, 1)]
    acc = None
    for n, (f, k, h) in enumerate(tiles):
        if f < 4:
            v = xin[f, k, pl.ds(8 * h, 8), :]
            m_st[0, f, pl.ds((G + 8 * h) * K + k, 8, stride=K), :] = v
        else:
            v = bm[pl.ds(G + 8 * h, 8), :]
        g = n % 16
        rolled = pltpu.roll(v, 4 + 8 * g, 1)
        acc = rolled if g == 0 else jnp.where(group8 == g, rolled, acc)
        if g == 15 or n == len(tiles) - 1:
            pack[pl.ds(8 * (n // 16), 8), :] = acc

    sign = jnp.where(top, -1.0, 1.0).astype(jnp.float32)
    lanes32 = lane((32, 128))
    turn32 = jnp.where(top, 127 - lanes32, lanes32)
    turn8 = jnp.where(top, 127 - lanes8, lanes8)
    sub8 = lax.broadcasted_iota(jnp.int32, (8, 128), 0)

    def turned(v, idx):
        return jnp.take_along_axis(v, idx, axis=1, mode="promise_in_bounds")

    edge = jnp.zeros((8, 128), jnp.float32)
    for d in range(1, G + 1):
        edge = jnp.where(sub8 == d - 1, bm[pl.ds(G + R - d, 1), :], edge)
    send_n[pl.ds(0, 8), :] = turned(edge, turn8)
    send_s[pl.ds(0, 8), :] = bm[pl.ds(G, 8), :]
    for d in range(1, G + 1):
        for f in range(4):
            at = HEAD + (d - 1) * 100 + f * K
            v = turned(m_st[0, f, pl.ds((G + R - d) * K, 32), :], turn32)
            if f >= 2:
                v = v * sign
            send_n[pl.ds(at, K), :] = v[:K]
            send_s[pl.ds(at, K), :] = m_st[0, f, pl.ds((G + d - 1) * K, K), :]

    pl.semaphore_wait(barrier, jnp.where(has_south, 4, 3))

    def remote(src, dst, ss, rs, to):
        return pltpu.make_async_remote_copy(
            src_ref=src, dst_ref=dst, send_sem=ss, recv_sem=rs, device_id=to, device_id_type=mesh_id
        )

    to_east = remote(pack, pack_w, lon_ss.at[0], lon_rs.at[0], {LON: east, LAT: j})
    to_west = remote(pack, pack_e, lon_ss.at[1], lon_rs.at[1], {LON: west, LAT: j})
    to_east.start()
    to_west.start()

    def row_pieces(q):
        if q < G:
            sl = pl.ds(*CHUNKS[q])
            return send_n.at[sl], send_s.at[sl], recv_n.at[sl], recv_s.at[sl]
        return csend_n, csend_s, crecv_n, crecv_s

    def start_rows(q):
        sn, ss, rn, rs = row_pieces(q)

        @pl.when(jnp.logical_not(top))
        def _():
            remote(sn, rs, n_ss.at[q], s_rs.at[q], north).start()

        @pl.when(top)
        def _():
            remote(sn, rn, n_ss.at[q], n_rs.at[q], north).start()

        @pl.when(has_south)
        def _():
            remote(ss, rn, s_ss.at[q], n_rs.at[q], south).start()

    def wait_rows(q):
        sn, ss, rn, rs = row_pieces(q)
        remote(ss, rn, s_ss.at[q], n_rs.at[q], north).wait_recv()

        @pl.when(has_south)
        def _():
            remote(sn, rs, n_ss.at[q], s_rs.at[q], south).wait_recv()

    def wait_sent(q):
        sn, ss, rn, rs = row_pieces(q)
        remote(sn, rs, n_ss.at[q], s_rs.at[q], north).wait_send()

        @pl.when(has_south)
        def _():
            remote(ss, rn, s_ss.at[q], n_rs.at[q], south).wait_send()

    start_rows(0)
    start_rows(1)

    @pl.when(jnp.logical_not(has_south))
    def _():
        zero = jnp.zeros((G * K, 128), jnp.float32)
        bm[pl.ds(0, G), :] = zero[:G]
        bq[pl.ds(0, G), :] = zero[:G]
        for f in range(4):
            m_st[0, f, pl.ds(0, G * K), :] = zero
            q_st[0, f, pl.ds(0, G * K), :] = zero

    to_east.wait_recv()
    to_west.wait_recv()
    west_half = lanes8 % 8 < 4
    for q in range(PACKED // 8):
        both = jnp.where(west_half, pack_w[pl.ds(8 * q, 8), :], pack_e[pl.ds(8 * q, 8), :])
        for g in range(16):
            n = 16 * q + g
            if n >= len(tiles):
                break
            f, k, h = tiles[n]
            v = pltpu.roll(both, (124 - 8 * g) % 128, 1)
            if f < 4:
                q_st[0, f, pl.ds((G + 8 * h) * K + k, 8, stride=K), :] = v
            else:
                bq[pl.ds(G + 8 * h, 8), :] = v

    flip8 = jnp.where(top, lanes8 + 7 - 2 * (lanes8 % 8), lanes8)
    sign8 = jnp.where(lanes8 >= 64, sign, 1.0)
    for d in range(1, G):
        acc_n = acc_s = None
        for g in range(16):
            f, kb = g // 4, KB[g % 4]
            vn = pltpu.roll(q_st[0, f, pl.ds((G + R - d) * K + kb, 8), :], 4 + 8 * g, 1)
            vs = pltpu.roll(q_st[0, f, pl.ds((G + d - 1) * K + kb, 8), :], 4 + 8 * g, 1)
            acc_n = vn if g == 0 else jnp.where(group8 == g, vn, acc_n)
            acc_s = vs if g == 0 else jnp.where(group8 == g, vs, acc_s)
        csend_n[pl.ds(8 * (d - 1), 8), :] = turned(acc_n, flip8) * sign8
        csend_s[pl.ds(8 * (d - 1), 8), :] = acc_s
    edge = jnp.zeros((8, 128), jnp.float32)
    for d in range(1, G + 1):
        edge = jnp.where(sub8 == d - 1, bq[pl.ds(G + R - d, 1), :], edge)
    csend_n[pl.ds(24, 8), :] = turned(pltpu.roll(edge, 4, 1), flip8)
    csend_s[pl.ds(24, 8), :] = pltpu.roll(bq[pl.ds(G, 8), :], 4, 1)
    start_rows(4)
    start_rows(2)
    start_rows(3)

    kk = lax.broadcasted_iota(jnp.int32, (32, 128), 0).astype(jnp.float32)
    first1 = lane((1, 128)) == 0
    last1 = lane((1, 128)) == 127
    firstb = lane((BLOCK, 128)) == 0
    lastb = lane((BLOCK, 128)) == 127
    total_rows = n_lat * R

    def masks(r):
        at = r * K
        bmc, bqc = bm[pl.ds(r, 1), :], bq[pl.ds(r, 1), :]
        me, mw = pltpu.roll(bmc, 127, 1), pltpu.roll(bmc, 1, 1)
        qe, qw = pltpu.roll(bqc, 127, 1), pltpu.roll(bqc, 1, 1)
        sides = (
            (mk, bmc, jnp.where(last1, qe, me), jnp.where(first1, qw, mw), bm),
            (qk, bqc, jnp.where(last1, me, qe), jnp.where(first1, mw, qw), bq),
        )
        for store, c, e, w, rows in sides:
            n, s = rows[pl.ds(r + 1, 1), :], rows[pl.ds(r - 1, 1), :]

            def flag(x):
                return jnp.where(kk < x, 1.0, 0.0)

            wet = flag(c)
            vu = jnp.where(kk >= 1.0, vertical_mixing * wet, 0.0)
            vd = vertical_mixing * flag(c - 1.0)
            drag = jnp.where(kk == c - 1.0, 1.0 - drag_rate, 1.0)
            for q, x in enumerate(
                (
                    flag(jnp.minimum(c, e)), flag(jnp.minimum(c, w)), flag(jnp.minimum(c, n)), flag(jnp.minimum(c, s)),
                    vu, vd, wet - vu - vd, wet * drag,
                )
            ):
                store[q, pl.ds(at, K), :] = x[:K]
        row = j * R + r - G
        row = jnp.where(row >= total_rows, 2 * total_rows - 1 - row, row)
        f = rotation * (2.0 * (row.astype(jnp.float32) + 0.5) / total_rows - 1.0)
        cor[pl.ds(at, K), :] = jnp.full((K, 128), 1.0, jnp.float32) * f

    def pressure(s, start, count, stride):
        for st, out in ((m_st, pm), (q_st, pq)):
            total = None
            for k in range(K):
                sl = pl.ds(start + k, count, stride=stride)
                x = density(st[s, 0, sl, :], st[s, 1, sl, :])
                total = x if total is None else total + x
                out[s, sl, :] = total

    def update(s, b, size, with_q, keep):
        first, last = firstb[:size], lastb[:size]
        sl = pl.ds(b, size)
        mc = [m_st[s, f, sl, :] for f in range(4)] + [pm[s, sl, :]]
        qc = [q_st[s, f, sl, :] for f in range(4)] + [pq[s, sl, :]]
        m_e, m_w, q_e, q_w = [], [], [], []
        for m, q in zip(mc, qc):
            me, mw = pltpu.roll(m, 127, 1), pltpu.roll(m, 1, 1)
            qe, qw = pltpu.roll(q, 127, 1), pltpu.roll(q, 1, 1)
            m_e.append(jnp.where(last, qe, me))
            m_w.append(jnp.where(first, qw, mw))
            if with_q:
                q_e.append(jnp.where(last, me, qe))
                q_w.append(jnp.where(first, mw, qw))
        work = [(m_st, pm, mk, mc, m_e, m_w)]
        if with_q:
            work.append((q_st, pq, qk, qc, q_e, q_w))
        for st, pr, mask, c, e, w in work:
            fe, fw, fn, fs, vu, vd, w0, wd = [mask[q, sl, :] for q in range(N_MASK)]
            a, b_ = courant * c[2], courant * c[3]
            a_neg, b_neg = jnp.minimum(a, 0.0), jnp.minimum(b_, 0.0)
            ce = fe * (mixing - a_neg)
            cw = fw * (mixing + (a - a_neg))
            cn = fn * (mixing - b_neg)
            cs = fs * (mixing + (b_ - b_neg))
            c0 = w0 - ((ce + cw) + (cn + cs))
            north_sl, south_sl = pl.ds(b + K, size), pl.ds(b - K, size)
            new = []
            for f in range(4):
                x = (c0 * c[f] + ce * e[f]) + (cw * w[f] + cn * st[s, f, north_sl, :])
                x = x + (cs * st[s, f, south_sl, :] + vu * st[s, f, pl.ds(b - 1, size), :])
                new.append(x + vd * st[s, f, pl.ds(b + 1, size), :])
            p = c[4]
            px = fe * (e[4] - p) + fw * (p - w[4])
            py = fn * (pr[s, north_sl, :] - p) + fs * (p - pr[s, south_sl, :])
            f0 = cor[sl, :]
            new[2] = wd * (new[2] + f0 * c[3] - px)
            new[3] = wd * (new[3] - f0 * c[2] - py)
            for f in range(4):
                if s < SWEEPS - 1:
                    st[s + 1, f, pl.ds(b, keep), :] = new[f][:keep]
                else:
                    m4[f, pl.ds(b - G * K, keep), :] = new[f][:keep]

    def mask_loop(lo, hi):
        def body(r, carry):
            masks(r)
            return carry

        lax.fori_loop(lo, hi, body, 0)

    mask_loop(G + 1, G + R - 1)
    for s in range(SWEEPS):
        count = R - 2 * s
        pressure(s, (G + s) * K, 8, K)
        pressure(s, (G + R - s - 8) * K, 8, K)
        lo, hi = (G + s + 1) * K, (G + R - s - 1) * K
        steps = -(-(hi - lo) // BLOCK)

        def body(t, carry, s=s, lo=lo, hi=hi):
            b = jnp.minimum(lo + t * BLOCK, hi - BLOCK)
            update(s, b, BLOCK, s < SWEEPS - 1, BLOCK)
            return carry

        lax.fori_loop(0, steps, body, 0)

    def unpack_rows(d):
        for f in range(4):
            src = pl.ds(HEAD + (d - 1) * 100 + f * K, K)
            m_st[0, f, pl.ds((G + R - 1 + d) * K, K), :] = recv_n[src, :]

        @pl.when(has_south)
        def _():
            for f in range(4):
                src = pl.ds(HEAD + (d - 1) * 100 + f * K, K)
                m_st[0, f, pl.ds((G - d) * K, K), :] = recv_s[src, :]

    def unpack_corner(src, row_of):
        edge = pltpu.roll(src[pl.ds(24, 8), :], 124, 1)
        for d in range(1, G + 1):
            bq[pl.ds(row_of(d), 1), :] = edge[d - 1 : d]
        for d in range(1, G):
            both = src[pl.ds(8 * (d - 1), 8), :]
            for g in range(16):
                f, kb = g // 4, KB[g % 4]
                q_st[0, f, pl.ds(row_of(d) * K + kb, 8), :] = pltpu.roll(both, (124 - 8 * g) % 128, 1)

    def north_row(d):
        return G + R - 1 + d

    def south_row(d):
        return G - d

    for e in range(1, G + 1):
        wait_rows(e - 1)
        unpack_rows(e)
        if e == 1:
            wait_rows(4)
            for d in range(1, G + 1):
                bm[pl.ds(north_row(d), 1), :] = recv_n[pl.ds(d - 1, 1), :]
            unpack_corner(crecv_n, north_row)

            @pl.when(has_south)
            def _():
                for d in range(1, G + 1):
                    bm[pl.ds(south_row(d), 1), :] = recv_s[pl.ds(d - 1, 1), :]
                unpack_corner(crecv_s, south_row)

            mask_loop(1, G + 1)
            mask_loop(G + R - 1, 2 * G + R - 1)
        for s in range(SWEEPS):
            d = e - s
            pressure(s, south_row(d) * K, 2, (north_row(d) - south_row(d)) * K)
            for row in (south_row(d - 1), north_row(d - 1)):
                update(s, row * K, 32, s < SWEEPS - 1 and e < G, K)

    done = pltpu.make_async_copy(m4, out_hbm, out_sem.at[0])
    done.start()
    to_east.wait_send()
    to_west.wait_send()
    for q in range(G + 1):
        wait_sent(q)
    done.wait()


def write_out(m4, t_out, s_out, u_out, v_out):
    for f, out in enumerate((t_out, s_out, u_out, v_out)):
        for k in range(K):
            for h in range(2):
                out[k, pl.ds(8 * h, 8), :] = m4[f, pl.ds(8 * h * K + k, 8, stride=K), :]


def per_device(n_lon, n_lat, t, s, u, v, water_indicator, bottom):
    del water_indicator
    f32 = jnp.float32
    hbm = pl.BlockSpec(memory_space=pl.ANY)
    vmem = pltpu.VMEM
    dma = pltpu.SemaphoreType.DMA
    states = pl.pallas_call(
        functools.partial(kernel, n_lon, n_lat),
        out_shape=jax.ShapeDtypeStruct((4, R * K, 128), f32),
        in_specs=[hbm] * 5,
        out_specs=hbm,
        scratch_shapes=[
            vmem((4, K, R, 128), f32), vmem((R, 128), jnp.int32),
            vmem((SWEEPS, 4, LIN, 128), f32), vmem((SWEEPS, 4, LIN, 128), f32), vmem((4, R * K, 128), f32),
            vmem((SWEEPS, LIN, 128), f32), vmem((SWEEPS, LIN, 128), f32),
            vmem((N_MASK, LIN, 128), f32), vmem((N_MASK, LIN, 128), f32), vmem((LIN, 128), f32),
            vmem((32, 128), f32), vmem((32, 128), f32),
            vmem((PACKED, 128), f32), vmem((PACKED, 128), f32), vmem((PACKED, 128), f32),
            vmem((MSG, 128), f32), vmem((MSG, 128), f32), vmem((MSG, 128), f32), vmem((MSG, 128), f32),
            vmem((CORNER, 128), f32), vmem((CORNER, 128), f32), vmem((CORNER, 128), f32), vmem((CORNER, 128), f32),
            dma((5,)), dma((1,)), dma((2,)), dma((2,)), dma((5,)), dma((5,)), dma((5,)), dma((5,)),
        ],
        compiler_params=pltpu.CompilerParams(
            collective_id=1, has_side_effects=True, vmem_limit_bytes=48 * 1024 * 1024
        ),
        name="sweeps",
    )(t, s, u, v, bottom)
    field = jax.ShapeDtypeStruct((K, R, 128), f32)
    return tuple(
        pl.pallas_call(
            write_out,
            out_shape=[field] * 4,
            compiler_params=pltpu.CompilerParams(vmem_limit_bytes=16 * 1024 * 1024),
            name="write_out",
        )(states)
    )


def solution(mesh):
    field = P(None, LAT, LON)
    return jax.shard_map(
        functools.partial(per_device, mesh.shape[LON], mesh.shape[LAT]),
        mesh=mesh,
        in_specs=(field,) * 5 + (P(LAT, LON),),
        out_specs=(field,) * 4,
        check_vma=False,
    )
```

profile of v0, /device:TPU:477, one launch (start us, length us, event | category | flops | bytes accessed | tf_op | source)
XLA Modules:
  0.0 32.9 jit_solution(10007566084860979324)
XLA Ops:
  0.6 0.0 copy-start
  0.6 0.9 %copy-done = f32[25,16,128]{2,1,0:T(8,128)S(1)} copy-done((f32[25,16,128]{2,1,0:T(8,128)S(1)}, f32[25,16,128]{2,1,0:T(8,128)}, u32[]{:S(2)}) %copy-start) | copy-done | bytes 204824
  1.6 0.0 copy-start.1
  1.6 0.9 %copy-done.1 = f32[25,16,128]{2,1,0:T(8,128)S(1)} copy-done((f32[25,16,128]{2,1,0:T(8,128)S(1)}, f32[25,16,128]{2,1,0:T(8,128)}, u32[]{:S(2)}) %copy-start.1) | copy-done | bytes 204824
  2.5 0.0 copy-start.2
  2.5 0.9 %copy-done.2 = f32[25,16,128]{2,1,0:T(8,128)S(1)} copy-done((f32[25,16,128]{2,1,0:T(8,128)S(1)}, f32[25,16,128]{2,1,0:T(8,128)}, u32[]{:S(2)}) %copy-start.2) | copy-done | bytes 204824
  3.4 0.0 copy-start.3
  3.4 0.9 %copy-done.3 = f32[25,16,128]{2,1,0:T(8,128)S(1)} copy-done((f32[25,16,128]{2,1,0:T(8,128)S(1)}, f32[25,16,128]{2,1,0:T(8,128)}, u32[]{:S(2)}) %copy-start.3) | copy-done | bytes 204824
  4.4 0.0 copy-start.4
  4.4 0.7 %copy-done.4 = s32[16,128]{1,0:T(8,128)S(1)} copy-done((s32[16,128]{1,0:T(8,128)S(1)}, s32[16,128]{1,0:T(8,128)}, u32[]{:S(2)}) %copy-start.4) | copy-done | bytes 8216
  5.1 26.9 %sweeps.1.m4 = f32[4,400,128]{2,1,0:T(8,128)S(1)} custom-call(f32[25,16,128]{2,1,0:T(8,128)S(1)} %copy-done, f32[25,16,128]{2,1,0:T(8,128)S(1)} %copy-done.1, f32[25,16,128]{2,1,0:T(8,128)S(1)} %copy-done.2, f32[25,16,128]{2,1,0:T(8,128)S(1)} %copy-done.3, s32[16,128]{1,0:T(8,128)S(1)} %copy-done.4), custom_call_target="tpu_custom_call" | custom-call | tf_op jit(solution)/shard_map/sweeps/pallas_call | solution.py:407
  32.0 0.9 %write_out.1 = (f32[25,16,128]{2,1,0:T(8,128)}, f32[25,16,128]{2,1,0:T(8,128)}, f32[25,16,128]{2,1,0:T(8,128)}, f32[25,16,128]{2,1,0:T(8,128)}) custom-call(f32[4,400,128]{2,1,0:T(8,128)S(1)} %sweeps.1.m4), custom_call_target="tpu_custom_call" | custom-call | tf_op jit(solution)/shard_map/write_out/pallas_call | solution.py:430
Async XLA Ops:
  0.6 0.9 %copy-start = (f32[25,16,128]{2,1,0:T(8,128)S(1)}, f32[25,16,128]{2,1,0:T(8,128)}, u32[]{:S(2)}) copy-start(f32[25,16,128]{2,1,0:T(8,128)} %t_hbm.1) | copy-start | bytes 614404
  1.6 0.9 %copy-start.1 = (f32[25,16,128]{2,1,0:T(8,128)S(1)}, f32[25,16,128]{2,1,0:T(8,128)}, u32[]{:S(2)}) copy-start(f32[25,16,128]{2,1,0:T(8,128)} %s_hbm.1) | copy-start | bytes 614404
  2.5 0.9 %copy-start.2 = (f32[25,16,128]{2,1,0:T(8,128)S(1)}, f32[25,16,128]{2,1,0:T(8,128)}, u32[]{:S(2)}) copy-start(f32[25,16,128]{2,1,0:T(8,128)} %u_hbm.1) | copy-start | bytes 614404
  3.4 0.9 %copy-start.3 = (f32[25,16,128]{2,1,0:T(8,128)S(1)}, f32[25,16,128]{2,1,0:T(8,128)}, u32[]{:S(2)}) copy-start(f32[25,16,128]{2,1,0:T(8,128)} %v_hbm.1) | copy-start | bytes 614404
  4.4 0.7 %copy-start.4 = (s32[16,128]{1,0:T(8,128)S(1)}, s32[16,128]{1,0:T(8,128)}, u32[]{:S(2)}) copy-start(s32[16,128]{1,0:T(8,128)} %b_hbm.1) | copy-start | bytes 24580
where the time goes:
time: 33.2 us; the launch traced here: 32.9 us
  Pallas kernels  27.8 us (84%)
  local copies, waits for them, and re-layouts  4.41 us (13%)
  between operations  0.65 us (2%)
    pallas_call x1, Pallas kernels, per_device(): pl.pallas_call(functools.partial(kernel, n_lon, n_lat), out_shape=jax.Sha...  26.9 us
    unnamed x10, local copies, waits for them, and re-layouts  4.41 us
    pallas_call x1, Pallas kernels, per_device(): pl.pallas_call(write_out, out_shape=[field] * 4, compiler_params=pltpu.Co...  0.94 us

commit v1 on v0

--- a/solution.py
+++ b/solution.py
@@ -45,10 +45,10 @@
 
 
 def kernel(
-    n_lon, n_lat, t_hbm, s_hbm, u_hbm, v_hbm, b_hbm, out_hbm,
-    xin, bin_, m_st, q_st, m4, pm, pq, mk, qk, cor, bm, bq,
+    n_lon, n_lat, t_hbm, s_hbm, u_hbm, v_hbm, b_hbm, m4,
+    xin, bin_, m_st, q_st, pm, pq, mk, qk, cor, bm, bq,
     pack, pack_w, pack_e, send_n, send_s, recv_n, recv_s, csend_n, csend_s, crecv_n, crecv_s,
-    in_sem, out_sem, lon_ss, lon_rs, n_ss, n_rs, s_ss, s_rs,
+    in_sem, lon_ss, lon_rs, n_ss, n_rs, s_ss, s_rs,
 ):
     i = lax.axis_index(LON)
     j = lax.axis_index(LAT)
@@ -382,13 +382,10 @@
             for row in (south_row(d - 1), north_row(d - 1)):
                 update(s, row * K, 32, s < SWEEPS - 1 and e < G, K)
 
-    done = pltpu.make_async_copy(m4, out_hbm, out_sem.at[0])
-    done.start()
     to_east.wait_send()
     to_west.wait_send()
     for q in range(G + 1):
         wait_sent(q)
-    done.wait()
 
 
 def write_out(m4, t_out, s_out, u_out, v_out):
@@ -406,25 +403,25 @@
     dma = pltpu.SemaphoreType.DMA
     states = pl.pallas_call(
         functools.partial(kernel, n_lon, n_lat),
-        out_shape=jax.ShapeDtypeStruct((4, R * K, 128), f32),
+        out_shape=pltpu.VMEM((4, R * K, 128), f32),
         in_specs=[hbm] * 5,
-        out_specs=hbm,
+        out_specs=pl.BlockSpec(memory_space=pltpu.VMEM),
         scratch_shapes=[
             vmem((4, K, R, 128), f32), vmem((R, 128), jnp.int32),
-            vmem((SWEEPS, 4, LIN, 128), f32), vmem((SWEEPS, 4, LIN, 128), f32), vmem((4, R * K, 128), f32),
+            vmem((SWEEPS, 4, LIN, 128), f32), vmem((SWEEPS, 4, LIN, 128), f32),
             vmem((SWEEPS, LIN, 128), f32), vmem((SWEEPS, LIN, 128), f32),
             vmem((N_MASK, LIN, 128), f32), vmem((N_MASK, LIN, 128), f32), vmem((LIN, 128), f32),
             vmem((32, 128), f32), vmem((32, 128), f32),
             vmem((PACKED, 128), f32), vmem((PACKED, 128), f32), vmem((PACKED, 128), f32),
             vmem((MSG, 128), f32), vmem((MSG, 128), f32), vmem((MSG, 128), f32), vmem((MSG, 128), f32),
             vmem((CORNER, 128), f32), vmem((CORNER, 128), f32), vmem((CORNER, 128), f32), vmem((CORNER, 128), f32),
-            dma((5,)), dma((1,)), dma((2,)), dma((2,)), dma((5,)), dma((5,)), dma((5,)), dma((5,)),
+            dma((5,)), dma((2,)), dma((2,)), dma((5,)), dma((5,)), dma((5,)), dma((5,)),
         ],
         compiler_params=pltpu.CompilerParams(
             collective_id=1, has_side_effects=True, vmem_limit_bytes=48 * 1024 * 1024
         ),
         name="sweeps",
-    )(t, s, u, v, bottom)
+    )(*(pltpu.with_memory_space_constraint(x, pltpu.HBM) for x in (t, s, u, v, bottom)))
     field = jax.ShapeDtypeStruct((K, R, 128), f32)
     return tuple(
         pl.pallas_call(

time: 33.2 us -> 28.5 us (0.86)
  local copies, waits for them, and re-layouts: 4.41 us -> 0 us
    unnamed x10 -> x0, local copies, waits for them, and re-layouts: 4.41 us -> none
where the time goes in v1:
time: 28.5 us; the launch traced here: 28.4 us
  Pallas kernels  27.7 us (97%)
  between operations  0.64 us (2%)
    pallas_call x1, Pallas kernels, per_device(): pl.pallas_call(functools.partial(kernel, n_lon, n_lat), out_shape=pltpu.V...  26.8 us
    pallas_call x1, Pallas kernels, per_device(): pl.pallas_call(write_out, out_shape=[field] * 4, compiler_params=pltpu.Co...  0.94 us

profile of v1, /device:TPU:477, one launch (start us, length us, event | category | flops | bytes accessed | tf_op | source)
XLA Modules:
  0.0 28.4 jit_solution(5877003947901296505)
XLA Ops:
  0.6 26.8 %sweeps.1.m4 = f32[4,400,128]{2,1,0:T(8,128)S(1)} custom-call(f32[25,16,128]{2,1,0:T(8,128)} %t_hbm.1, f32[25,16,128]{2,1,0:T(8,128)} %s_hbm.1, f32[25,16,128]{2,1,0:T(8,128)} %u_hbm.1, f32[25,16,128]{2,1,0:T(8,128)} %v_hbm.1, s32[16,128]{1,0:T(8,128)} %b_hbm.1), custom_call_target="tpu_custom_call" | custom-call | tf_op jit(solution)/shard_map/sweeps/pallas_call | solution.py:404
  27.4 0.9 %write_out.1 = (f32[25,16,128]{2,1,0:T(8,128)}, f32[25,16,128]{2,1,0:T(8,128)}, f32[25,16,128]{2,1,0:T(8,128)}, f32[25,16,128]{2,1,0:T(8,128)}) custom-call(f32[4,400,128]{2,1,0:T(8,128)S(1)} %sweeps.1.m4), custom_call_target="tpu_custom_call" | custom-call | tf_op jit(solution)/shard_map/write_out/pallas_call | solution.py:427

commit v2 on v1

--- a/solution.py
+++ b/solution.py
@@ -46,9 +46,9 @@
 
 def kernel(
     n_lon, n_lat, t_hbm, s_hbm, u_hbm, v_hbm, b_hbm, m4,
-    xin, bin_, m_st, q_st, pm, pq, mk, qk, cor, bm, bq,
-    pack, pack_w, pack_e, send_n, send_s, recv_n, recv_s, csend_n, csend_s, crecv_n, crecv_s,
-    in_sem, lon_ss, lon_rs, n_ss, n_rs, s_ss, s_rs,
+    xin, bin_, m_st, q_st, pm, pq, mk, qk, cor, bm, bq, b_side,
+    pack, pack_w, pack_e, send_n, send_s, recv_n, recv_s, passing, csend_n, csend_s, crecv_n, crecv_s,
+    in_sem, lon_ss, lon_rs, n_ss, n_rs, s_ss, s_rs, pass_ss, pass_rs,
 ):
     i = lax.axis_index(LON)
     j = lax.axis_index(LAT)
@@ -59,6 +59,10 @@
     north = {LON: jnp.where(top, n_lon - 1 - i, i), LAT: jnp.where(top, j, j + 1)}
     south = {LON: i, LAT: jnp.maximum(j - 1, 0)}
     mesh_id = pl.DeviceIdType.MESH
+    relays = j == n_lat - 2
+    across = lax.rem(i + n_lon // 2, n_lon)
+    relay = {LON: across, LAT: jnp.maximum(n_lat - 2, 0)}
+    relayed = {LON: across, LAT: n_lat - 1}
 
     barrier = pltpu.get_barrier_semaphore()
     pl.semaphore_signal(barrier, inc=1, device_id={LON: east, LAT: j}, device_id_type=mesh_id)
@@ -68,6 +72,14 @@
     @pl.when(has_south)
     def _():
         pl.semaphore_signal(barrier, inc=1, device_id=south, device_id_type=mesh_id)
+
+    @pl.when(jnp.logical_or(top, relays))
+    def _():
+        pl.semaphore_signal(barrier, inc=1, device_id=relay, device_id_type=mesh_id)
+
+    @pl.when(relays)
+    def _():
+        pl.semaphore_signal(barrier, inc=1, device_id=relayed, device_id_type=mesh_id)
 
     loads = [
         pltpu.make_async_copy(ref, xin.at[f], in_sem.at[f])
@@ -121,7 +133,7 @@
             send_n[pl.ds(at, K), :] = v[:K]
             send_s[pl.ds(at, K), :] = m_st[0, f, pl.ds((G + d - 1) * K, K), :]
 
-    pl.semaphore_wait(barrier, jnp.where(has_south, 4, 3))
+    pl.semaphore_wait(barrier, jnp.where(has_south, 4, 3) + jnp.where(top, 1, 0) + jnp.where(relays, 2, 0))
 
     def remote(src, dst, ss, rs, to):
         return pltpu.make_async_remote_copy(
@@ -150,9 +162,17 @@
         def _():
             remote(sn, rn, n_ss.at[q], n_rs.at[q], north).start()
 
-        @pl.when(has_south)
+        direct = has_south if q == G else jnp.logical_and(has_south, jnp.logical_not(top))
+
+        @pl.when(direct)
         def _():
             remote(ss, rn, s_ss.at[q], n_rs.at[q], south).start()
+
+        if q < G:
+
+            @pl.when(top)
+            def _():
+                remote(ss, passing.at[pl.ds(*CHUNKS[q])], s_ss.at[q], pass_rs.at[q], relay).start()
 
     def wait_rows(q):
         sn, ss, rn, rs = row_pieces(q)
@@ -161,6 +181,17 @@
         @pl.when(has_south)
         def _():
             remote(sn, rs, n_ss.at[q], s_rs.at[q], south).wait_recv()
+
+    def passed(q):
+        sl = pl.ds(*CHUNKS[q])
+        return remote(passing.at[sl], recv_n.at[sl], pass_ss.at[q], n_rs.at[q], relay)
+
+    def pass_on(q):
+        @pl.when(relays)
+        def _():
+            sl = pl.ds(*CHUNKS[q])
+            remote(send_s.at[sl], passing.at[sl], s_ss.at[q], pass_rs.at[q], relay).wait_recv()
+            passed(q).start()
 
     def wait_sent(q):
         sn, ss, rn, rs = row_pieces(q)
@@ -218,22 +249,30 @@
     start_rows(4)
     start_rows(2)
     start_rows(3)
+    pass_on(0)
+    pass_on(1)
 
     kk = lax.broadcasted_iota(jnp.int32, (32, 128), 0).astype(jnp.float32)
-    first1 = lane((1, 128)) == 0
-    last1 = lane((1, 128)) == 127
     firstb = lane((BLOCK, 128)) == 0
     lastb = lane((BLOCK, 128)) == 127
     total_rows = n_lat * R
 
+    def sides_of_bottom(rows):
+        for r in rows:
+            sl = pl.ds(r, 8)
+            m, q = bm[sl, :], bq[sl, :]
+            first, last = lanes8 == 0, lanes8 == 127
+            b_side[0, sl, :] = pltpu.roll(jnp.where(first, q, m), 127, 1)
+            b_side[1, sl, :] = pltpu.roll(jnp.where(last, q, m), 1, 1)
+            b_side[2, sl, :] = pltpu.roll(jnp.where(first, m, q), 127, 1)
+            b_side[3, sl, :] = pltpu.roll(jnp.where(last, m, q), 1, 1)
+
     def masks(r):
         at = r * K
-        bmc, bqc = bm[pl.ds(r, 1), :], bq[pl.ds(r, 1), :]
-        me, mw = pltpu.roll(bmc, 127, 1), pltpu.roll(bmc, 1, 1)
-        qe, qw = pltpu.roll(bqc, 127, 1), pltpu.roll(bqc, 1, 1)
+        one = pl.ds(r, 1)
         sides = (
-            (mk, bmc, jnp.where(last1, qe, me), jnp.where(first1, qw, mw), bm),
-            (qk, bqc, jnp.where(last1, me, qe), jnp.where(first1, mw, qw), bq),
+            (mk, bm[one, :], b_side[0, one, :], b_side[1, one, :], bm),
+            (qk, bq[one, :], b_side[2, one, :], b_side[3, one, :], bq),
         )
         for store, c, e, w, rows in sides:
             n, s = rows[pl.ds(r + 1, 1), :], rows[pl.ds(r - 1, 1), :]
@@ -317,6 +356,7 @@
 
         lax.fori_loop(lo, hi, body, 0)
 
+    sides_of_bottom((G, G + 8))
     mask_loop(G + 1, G + R - 1)
     for s in range(SWEEPS):
         count = R - 2 * s
@@ -331,6 +371,8 @@
             return carry
 
         lax.fori_loop(0, steps, body, 0)
+        if s in (0, 1):
+            pass_on(s + 2)
 
     def unpack_rows(d):
         for f in range(4):
@@ -359,31 +401,48 @@
     def south_row(d):
         return G - d
 
-    for e in range(1, G + 1):
-        wait_rows(e - 1)
-        unpack_rows(e)
-        if e == 1:
-            wait_rows(4)
-            for d in range(1, G + 1):
-                bm[pl.ds(north_row(d), 1), :] = recv_n[pl.ds(d - 1, 1), :]
-            unpack_corner(crecv_n, north_row)
-
-            @pl.when(has_south)
-            def _():
-                for d in range(1, G + 1):
-                    bm[pl.ds(south_row(d), 1), :] = recv_s[pl.ds(d - 1, 1), :]
-                unpack_corner(crecv_s, south_row)
-
-            mask_loop(1, G + 1)
-            mask_loop(G + R - 1, 2 * G + R - 1)
-        for s in range(SWEEPS):
-            d = e - s
-            pressure(s, south_row(d) * K, 2, (north_row(d) - south_row(d)) * K)
-            for row in (south_row(d - 1), north_row(d - 1)):
-                update(s, row * K, 32, s < SWEEPS - 1 and e < G, K)
+    wait_rows(0)
+    wait_rows(4)
+    for d in range(1, G + 1):
+        bm[pl.ds(north_row(d), 1), :] = recv_n[pl.ds(d - 1, 1), :]
+    unpack_corner(crecv_n, north_row)
+
+    @pl.when(has_south)
+    def _():
+        for d in range(1, G + 1):
+            bm[pl.ds(south_row(d), 1), :] = recv_s[pl.ds(d - 1, 1), :]
+        unpack_corner(crecv_s, south_row)
+
+    sides_of_bottom((0, 16))
+    mask_loop(1, G + 1)
+    mask_loop(G + R - 1, 2 * G + R - 1)
+    for d in range(1, G):
+        if d > 1:
+            wait_rows(d - 1)
+        unpack_rows(d)
+    for s in range(SWEEPS):
+        for row in (south_row(G - 1 - s), north_row(1 - s)):
+            pressure(s, row * K, 3, K)
+        for row in (south_row(2 - s), north_row(-s)):
+            for b in (row * K, row * K + 35):
+                update(s, b, 40, s < SWEEPS - 1, 40)
+
+    wait_rows(G - 1)
+    unpack_rows(G)
+    for s in range(SWEEPS):
+        d = G - s
+        pressure(s, south_row(d) * K, 2, (north_row(d) - south_row(d)) * K)
+        for row in (south_row(d - 1), north_row(d - 1)):
+            update(s, row * K, 32, False, K)
 
     to_east.wait_send()
     to_west.wait_send()
+    for q in range(G):
+
+        @pl.when(relays)
+        def _():
+            passed(q).wait_send()
+
     for q in range(G + 1):
         wait_sent(q)
 
@@ -411,11 +470,11 @@
             vmem((SWEEPS, 4, LIN, 128), f32), vmem((SWEEPS, 4, LIN, 128), f32),
             vmem((SWEEPS, LIN, 128), f32), vmem((SWEEPS, LIN, 128), f32),
             vmem((N_MASK, LIN, 128), f32), vmem((N_MASK, LIN, 128), f32), vmem((LIN, 128), f32),
-            vmem((32, 128), f32), vmem((32, 128), f32),
+            vmem((32, 128), f32), vmem((32, 128), f32), vmem((4, 32, 128), f32),
             vmem((PACKED, 128), f32), vmem((PACKED, 128), f32), vmem((PACKED, 128), f32),
-            vmem((MSG, 128), f32), vmem((MSG, 128), f32), vmem((MSG, 128), f32), vmem((MSG, 128), f32),
+            *[vmem((MSG, 128), f32)] * 5,
             vmem((CORNER, 128), f32), vmem((CORNER, 128), f32), vmem((CORNER, 128), f32), vmem((CORNER, 128), f32),
-            dma((5,)), dma((2,)), dma((2,)), dma((5,)), dma((5,)), dma((5,)), dma((5,)),
+            dma((5,)), dma((2,)), dma((2,)), dma((5,)), dma((5,)), dma((5,)), dma((5,)), dma((G,)), dma((G,)),
         ],
         compiler_params=pltpu.CompilerParams(
             collective_id=1, has_side_effects=True, vmem_limit_bytes=48 * 1024 * 1024

time: 28.5 us -> 29 us (1.018)
  the two profiles are of different devices: /device:TPU:477 before, /device:TPU:473 now
where the time goes in v2:
time: 29 us; the launch traced here: 28.8 us
  Pallas kernels  28.2 us (97%)
  between operations  0.64 us (2%)
    pallas_call x1, Pallas kernels, per_device(): pl.pallas_call(functools.partial(kernel, n_lon, n_lat), out_shape=pltpu.V...  27.3 us
    pallas_call x1, Pallas kernels, per_device(): pl.pallas_call(write_out, out_shape=[field] * 4, compiler_params=pltpu.Co...  0.94 us

profile of v2, /device:TPU:473, one launch (start us, length us, event | category | flops | bytes accessed | tf_op | source)
XLA Modules:
  0.0 28.8 jit_solution(10803282784473353728)
XLA Ops:
  0.6 27.3 %sweeps.1.m4 = f32[4,400,128]{2,1,0:T(8,128)S(1)} custom-call(f32[25,16,128]{2,1,0:T(8,128)} %t_hbm.1, f32[25,16,128]{2,1,0:T(8,128)} %s_hbm.1, f32[25,16,128]{2,1,0:T(8,128)} %u_hbm.1, f32[25,16,128]{2,1,0:T(8,128)} %v_hbm.1, s32[16,128]{1,0:T(8,128)} %b_hbm.1), custom_call_target="tpu_custom_call" | custom-call | tf_op jit(solution)/shard_map/sweeps/pallas_call | solution.py:463
  27.9 0.9 %write_out.1 = (f32[25,16,128]{2,1,0:T(8,128)}, f32[25,16,128]{2,1,0:T(8,128)}, f32[25,16,128]{2,1,0:T(8,128)}, f32[25,16,128]{2,1,0:T(8,128)}) custom-call(f32[4,400,128]{2,1,0:T(8,128)S(1)} %sweeps.1.m4), custom_call_target="tpu_custom_call" | custom-call | tf_op jit(solution)/shard_map/write_out/pallas_call | solution.py:486

commit v3 on v2

--- a/solution.py
+++ b/solution.py
@@ -59,10 +59,8 @@
     north = {LON: jnp.where(top, n_lon - 1 - i, i), LAT: jnp.where(top, j, j + 1)}
     south = {LON: i, LAT: jnp.maximum(j - 1, 0)}
     mesh_id = pl.DeviceIdType.MESH
-    relays = j == n_lat - 2
-    across = lax.rem(i + n_lon // 2, n_lon)
-    relay = {LON: across, LAT: jnp.maximum(n_lat - 2, 0)}
-    relayed = {LON: across, LAT: n_lat - 1}
+    across = {LON: lax.rem(i + n_lon // 2, n_lon), LAT: j}
+    relay = {LON: n_lon - 1 - lax.rem(i + n_lon // 2, n_lon), LAT: j}
 
     barrier = pltpu.get_barrier_semaphore()
     pl.semaphore_signal(barrier, inc=1, device_id={LON: east, LAT: j}, device_id_type=mesh_id)
@@ -73,13 +71,10 @@
     def _():
         pl.semaphore_signal(barrier, inc=1, device_id=south, device_id_type=mesh_id)
 
-    @pl.when(jnp.logical_or(top, relays))
+    @pl.when(top)
     def _():
+        pl.semaphore_signal(barrier, inc=1, device_id=across, device_id_type=mesh_id)
         pl.semaphore_signal(barrier, inc=1, device_id=relay, device_id_type=mesh_id)
-
-    @pl.when(relays)
-    def _():
-        pl.semaphore_signal(barrier, inc=1, device_id=relayed, device_id_type=mesh_id)
 
     loads = [
         pltpu.make_async_copy(ref, xin.at[f], in_sem.at[f])
@@ -133,7 +128,7 @@
             send_n[pl.ds(at, K), :] = v[:K]
             send_s[pl.ds(at, K), :] = m_st[0, f, pl.ds((G + d - 1) * K, K), :]
 
-    pl.semaphore_wait(barrier, jnp.where(has_south, 4, 3) + jnp.where(top, 1, 0) + jnp.where(relays, 2, 0))
+    pl.semaphore_wait(barrier, jnp.where(has_south, 4, 3) + jnp.where(top, 2, 0))
 
     def remote(src, dst, ss, rs, to):
         return pltpu.make_async_remote_copy(
@@ -151,28 +146,30 @@
             return send_n.at[sl], send_s.at[sl], recv_n.at[sl], recv_s.at[sl]
         return csend_n, csend_s, crecv_n, crecv_s
 
+    def start_north(q):
+        sn, ss, rn, rs = row_pieces(q)
+
+        @pl.when(jnp.logical_not(top))
+        def _():
+            remote(sn, rs, n_ss.at[q], s_rs.at[q], north).start()
+
+        @pl.when(top)
+        def _():
+            if q == G:
+                remote(sn, rn, n_ss.at[q], n_rs.at[q], north).start()
+            else:
+                remote(sn, passing.at[pl.ds(*CHUNKS[q])], n_ss.at[q], pass_rs.at[q], relay).start()
+
+    def start_south(q):
+        sn, ss, rn, rs = row_pieces(q)
+
+        @pl.when(has_south)
+        def _():
+            remote(ss, rn, s_ss.at[q], n_rs.at[q], south).start()
+
     def start_rows(q):
-        sn, ss, rn, rs = row_pieces(q)
-
-        @pl.when(jnp.logical_not(top))
-        def _():
-            remote(sn, rs, n_ss.at[q], s_rs.at[q], north).start()
-
-        @pl.when(top)
-        def _():
-            remote(sn, rn, n_ss.at[q], n_rs.at[q], north).start()
-
-        direct = has_south if q == G else jnp.logical_and(has_south, jnp.logical_not(top))
-
-        @pl.when(direct)
-        def _():
-            remote(ss, rn, s_ss.at[q], n_rs.at[q], south).start()
-
-        if q < G:
-
-            @pl.when(top)
-            def _():
-                remote(ss, passing.at[pl.ds(*CHUNKS[q])], s_ss.at[q], pass_rs.at[q], relay).start()
+        start_north(q)
+        start_south(q)
 
     def wait_rows(q):
         sn, ss, rn, rs = row_pieces(q)
@@ -184,13 +181,13 @@
 
     def passed(q):
         sl = pl.ds(*CHUNKS[q])
-        return remote(passing.at[sl], recv_n.at[sl], pass_ss.at[q], n_rs.at[q], relay)
+        return remote(passing.at[sl], recv_n.at[sl], pass_ss.at[q], n_rs.at[q], across)
 
     def pass_on(q):
-        @pl.when(relays)
+        @pl.when(top)
         def _():
             sl = pl.ds(*CHUNKS[q])
-            remote(send_s.at[sl], passing.at[sl], s_ss.at[q], pass_rs.at[q], relay).wait_recv()
+            remote(send_n.at[sl], passing.at[sl], n_ss.at[q], pass_rs.at[q], relay).wait_recv()
             passed(q).start()
 
     def wait_sent(q):
@@ -247,10 +244,12 @@
     csend_n[pl.ds(24, 8), :] = turned(pltpu.roll(edge, 4, 1), flip8)
     csend_s[pl.ds(24, 8), :] = pltpu.roll(bq[pl.ds(G, 8), :], 4, 1)
     start_rows(4)
-    start_rows(2)
-    start_rows(3)
+    start_north(2)
+    start_north(3)
     pass_on(0)
     pass_on(1)
+    start_south(2)
+    start_south(3)
 
     kk = lax.broadcasted_iota(jnp.int32, (32, 128), 0).astype(jnp.float32)
     firstb = lane((BLOCK, 128)) == 0
@@ -439,7 +438,7 @@
     to_west.wait_send()
     for q in range(G):
 
-        @pl.when(relays)
+        @pl.when(top)
         def _():
             passed(q).wait_send()
 

time: 29 us -> 29.5 us (1.017)
  the two profiles are of different devices: /device:TPU:473 before, /device:TPU:477 now
where the time goes in v3:
time: 29.5 us; the launch traced here: 29.3 us
  Pallas kernels  28.7 us (97%)
  between operations  0.64 us (2%)
    pallas_call x1, Pallas kernels, per_device(): pl.pallas_call(functools.partial(kernel, n_lon, n_lat), out_shape=pltpu.V...  27.7 us
    pallas_call x1, Pallas kernels, per_device(): pl.pallas_call(write_out, out_shape=[field] * 4, compiler_params=pltpu.Co...  0.94 us

profile of v3, /device:TPU:477, one launch (start us, length us, event | category | flops | bytes accessed | tf_op | source)
XLA Modules:
  0.0 29.3 jit_solution(720139300831408050)
XLA Ops:
  0.6 27.7 %sweeps.1.m4 = f32[4,400,128]{2,1,0:T(8,128)S(1)} custom-call(f32[25,16,128]{2,1,0:T(8,128)} %t_hbm.1, f32[25,16,128]{2,1,0:T(8,128)} %s_hbm.1, f32[25,16,128]{2,1,0:T(8,128)} %u_hbm.1, f32[25,16,128]{2,1,0:T(8,128)} %v_hbm.1, s32[16,128]{1,0:T(8,128)} %b_hbm.1), custom_call_target="tpu_custom_call" | custom-call | tf_op jit(solution)/shard_map/sweeps/pallas_call | solution.py:462
  28.4 0.9 %write_out.1 = (f32[25,16,128]{2,1,0:T(8,128)}, f32[25,16,128]{2,1,0:T(8,128)}, f32[25,16,128]{2,1,0:T(8,128)}, f32[25,16,128]{2,1,0:T(8,128)}) custom-call(f32[4,400,128]{2,1,0:T(8,128)S(1)} %sweeps.1.m4), custom_call_target="tpu_custom_call" | custom-call | tf_op jit(solution)/shard_map/write_out/pallas_call | solution.py:485

commit v4 on v3

--- a/solution.py
+++ b/solution.py
@@ -59,8 +59,13 @@
     north = {LON: jnp.where(top, n_lon - 1 - i, i), LAT: jnp.where(top, j, j + 1)}
     south = {LON: i, LAT: jnp.maximum(j - 1, 0)}
     mesh_id = pl.DeviceIdType.MESH
-    across = {LON: lax.rem(i + n_lon // 2, n_lon), LAT: j}
-    relay = {LON: n_lon - 1 - lax.rem(i + n_lon // 2, n_lon), LAT: j}
+    passes = j == 1
+    half_on = lax.rem(i + n_lon // 2, n_lon)
+    mirrored = n_lon - 1 - i
+    fold_to = {LON: half_on, LAT: jnp.int32(1)}
+    fold_from = {LON: lax.rem(mirrored + n_lon // 2, n_lon), LAT: jnp.int32(1)}
+    pass_from = {LON: half_on, LAT: jnp.int32(n_lat - 1)}
+    pass_to = {LON: n_lon - 1 - half_on, LAT: jnp.int32(n_lat - 1)}
 
     barrier = pltpu.get_barrier_semaphore()
     pl.semaphore_signal(barrier, inc=1, device_id={LON: east, LAT: j}, device_id_type=mesh_id)
@@ -71,10 +76,12 @@
     def _():
         pl.semaphore_signal(barrier, inc=1, device_id=south, device_id_type=mesh_id)
 
-    @pl.when(top)
-    def _():
-        pl.semaphore_signal(barrier, inc=1, device_id=across, device_id_type=mesh_id)
-        pl.semaphore_signal(barrier, inc=1, device_id=relay, device_id_type=mesh_id)
+    for here, first, second in ((top, fold_to, fold_from), (passes, pass_from, pass_to)):
+
+        @pl.when(here)
+        def _(first=first, second=second):
+            pl.semaphore_signal(barrier, inc=1, device_id=first, device_id_type=mesh_id)
+            pl.semaphore_signal(barrier, inc=1, device_id=second, device_id_type=mesh_id)
 
     loads = [
         pltpu.make_async_copy(ref, xin.at[f], in_sem.at[f])
@@ -128,7 +135,7 @@
             send_n[pl.ds(at, K), :] = v[:K]
             send_s[pl.ds(at, K), :] = m_st[0, f, pl.ds((G + d - 1) * K, K), :]
 
-    pl.semaphore_wait(barrier, jnp.where(has_south, 4, 3) + jnp.where(top, 2, 0))
+    pl.semaphore_wait(barrier, jnp.where(has_south, 4, 3) + jnp.where(jnp.logical_or(top, passes), 2, 0))
 
     def remote(src, dst, ss, rs, to):
         return pltpu.make_async_remote_copy(
@@ -158,7 +165,7 @@
             if q == G:
                 remote(sn, rn, n_ss.at[q], n_rs.at[q], north).start()
             else:
-                remote(sn, passing.at[pl.ds(*CHUNKS[q])], n_ss.at[q], pass_rs.at[q], relay).start()
+                remote(sn, passing.at[pl.ds(*CHUNKS[q])], n_ss.at[q], pass_rs.at[q], fold_to).start()
 
     def start_south(q):
         sn, ss, rn, rs = row_pieces(q)
@@ -181,13 +188,13 @@
 
     def passed(q):
         sl = pl.ds(*CHUNKS[q])
-        return remote(passing.at[sl], recv_n.at[sl], pass_ss.at[q], n_rs.at[q], across)
+        return remote(passing.at[sl], recv_n.at[sl], pass_ss.at[q], n_rs.at[q], pass_to)
 
     def pass_on(q):
-        @pl.when(top)
+        @pl.when(passes)
         def _():
             sl = pl.ds(*CHUNKS[q])
-            remote(send_n.at[sl], passing.at[sl], n_ss.at[q], pass_rs.at[q], relay).wait_recv()
+            remote(send_n.at[sl], passing.at[sl], n_ss.at[q], pass_rs.at[q], pass_from).wait_recv()
             passed(q).start()
 
     def wait_sent(q):
@@ -438,7 +445,7 @@
     to_west.wait_send()
     for q in range(G):
 
-        @pl.when(top)
+        @pl.when(passes)
         def _():
             passed(q).wait_send()
 

time: 29.5 us -> 32.9 us (1.12)
  the two profiles are of different devices: /device:TPU:477 before, /device:TPU:13 now
where the time goes in v4:
time: 32.9 us; the launch traced here: 32.7 us
  Pallas kernels  32.1 us (98%)
  between operations  0.64 us (2%)
    pallas_call x1, Pallas kernels, per_device(): pl.pallas_call(functools.partial(kernel, n_lon, n_lat), out_shape=pltpu.V...  31.2 us
    pallas_call x1, Pallas kernels, per_device(): pl.pallas_call(write_out, out_shape=[field] * 4, compiler_params=pltpu.Co...  0.94 us

profile of v4, /device:TPU:13, one launch (start us, length us, event | category | flops | bytes accessed | tf_op | source)
XLA Modules:
  0.0 32.7 jit_solution(16307059660588742687)
XLA Ops:
  0.6 31.2 %sweeps.1.m4 = f32[4,400,128]{2,1,0:T(8,128)S(1)} custom-call(f32[25,16,128]{2,1,0:T(8,128)} %t_hbm.1, f32[25,16,128]{2,1,0:T(8,128)} %s_hbm.1, f32[25,16,128]{2,1,0:T(8,128)} %u_hbm.1, f32[25,16,128]{2,1,0:T(8,128)} %v_hbm.1, s32[16,128]{1,0:T(8,128)} %b_hbm.1), custom_call_target="tpu_custom_call" | custom-call | tf_op jit(solution)/shard_map/sweeps/pallas_call | solution.py:469
  31.8 0.9 %write_out.1 = (f32[25,16,128]{2,1,0:T(8,128)}, f32[25,16,128]{2,1,0:T(8,128)}, f32[25,16,128]{2,1,0:T(8,128)}, f32[25,16,128]{2,1,0:T(8,128)}) custom-call(f32[4,400,128]{2,1,0:T(8,128)S(1)} %sweeps.1.m4), custom_call_target="tpu_custom_call" | custom-call | tf_op jit(solution)/shard_map/write_out/pallas_call | solution.py:492

commit v5 on v1

--- a/solution.py
+++ b/solution.py
@@ -46,7 +46,7 @@
 
 def kernel(
     n_lon, n_lat, t_hbm, s_hbm, u_hbm, v_hbm, b_hbm, m4,
-    xin, bin_, m_st, q_st, pm, pq, mk, qk, cor, bm, bq,
+    xin, bin_, m_st, q_st, pm, pq, mk, qk, cor, bm, bq, b_side,
     pack, pack_w, pack_e, send_n, send_s, recv_n, recv_s, csend_n, csend_s, crecv_n, crecv_s,
     in_sem, lon_ss, lon_rs, n_ss, n_rs, s_ss, s_rs,
 ):
@@ -220,20 +220,26 @@
     start_rows(3)
 
     kk = lax.broadcasted_iota(jnp.int32, (32, 128), 0).astype(jnp.float32)
-    first1 = lane((1, 128)) == 0
-    last1 = lane((1, 128)) == 127
     firstb = lane((BLOCK, 128)) == 0
     lastb = lane((BLOCK, 128)) == 127
     total_rows = n_lat * R
 
+    def sides_of_bottom(rows):
+        for r in rows:
+            sl = pl.ds(r, 8)
+            m, q = bm[sl, :], bq[sl, :]
+            first, last = lanes8 == 0, lanes8 == 127
+            b_side[0, sl, :] = pltpu.roll(jnp.where(first, q, m), 127, 1)
+            b_side[1, sl, :] = pltpu.roll(jnp.where(last, q, m), 1, 1)
+            b_side[2, sl, :] = pltpu.roll(jnp.where(first, m, q), 127, 1)
+            b_side[3, sl, :] = pltpu.roll(jnp.where(last, m, q), 1, 1)
+
     def masks(r):
         at = r * K
-        bmc, bqc = bm[pl.ds(r, 1), :], bq[pl.ds(r, 1), :]
-        me, mw = pltpu.roll(bmc, 127, 1), pltpu.roll(bmc, 1, 1)
-        qe, qw = pltpu.roll(bqc, 127, 1), pltpu.roll(bqc, 1, 1)
+        one = pl.ds(r, 1)
         sides = (
-            (mk, bmc, jnp.where(last1, qe, me), jnp.where(first1, qw, mw), bm),
-            (qk, bqc, jnp.where(last1, me, qe), jnp.where(first1, mw, qw), bq),
+            (mk, bm[one, :], b_side[0, one, :], b_side[1, one, :], bm),
+            (qk, bq[one, :], b_side[2, one, :], b_side[3, one, :], bq),
         )
         for store, c, e, w, rows in sides:
             n, s = rows[pl.ds(r + 1, 1), :], rows[pl.ds(r - 1, 1), :]
@@ -317,6 +323,7 @@
 
         lax.fori_loop(lo, hi, body, 0)
 
+    sides_of_bottom((G, G + 8))
     mask_loop(G + 1, G + R - 1)
     for s in range(SWEEPS):
         count = R - 2 * s
@@ -374,6 +381,7 @@
                     bm[pl.ds(south_row(d), 1), :] = recv_s[pl.ds(d - 1, 1), :]
                 unpack_corner(crecv_s, south_row)
 
+            sides_of_bottom((0, 16))
             mask_loop(1, G + 1)
             mask_loop(G + R - 1, 2 * G + R - 1)
         for s in range(SWEEPS):
@@ -411,7 +419,7 @@
             vmem((SWEEPS, 4, LIN, 128), f32), vmem((SWEEPS, 4, LIN, 128), f32),
             vmem((SWEEPS, LIN, 128), f32), vmem((SWEEPS, LIN, 128), f32),
             vmem((N_MASK, LIN, 128), f32), vmem((N_MASK, LIN, 128), f32), vmem((LIN, 128), f32),
-            vmem((32, 128), f32), vmem((32, 128), f32),
+            vmem((32, 128), f32), vmem((32, 128), f32), vmem((4, 32, 128), f32),
             vmem((PACKED, 128), f32), vmem((PACKED, 128), f32), vmem((PACKED, 128), f32),
             vmem((MSG, 128), f32), vmem((MSG, 128), f32), vmem((MSG, 128), f32), vmem((MSG, 128), f32),
             vmem((CORNER, 128), f32), vmem((CORNER, 128), f32), vmem((CORNER, 128), f32), vmem((CORNER, 128), f32),

time: 28.5 us -> 27.8 us (0.975)
  the two profiles are of different devices: /device:TPU:477 before, /device:TPU:449 now
where the time goes in v5:
time: 27.8 us; the launch traced here: 27.7 us
  Pallas kernels  27.1 us (97%)
  between operations  0.64 us (2%)
    pallas_call x1, Pallas kernels, per_device(): pl.pallas_call(functools.partial(kernel, n_lon, n_lat), out_shape=pltpu.V...  26.1 us
    pallas_call x1, Pallas kernels, per_device(): pl.pallas_call(write_out, out_shape=[field] * 4, compiler_params=pltpu.Co...  0.94 us

profile of v5, /device:TPU:449, one launch (start us, length us, event | category | flops | bytes accessed | tf_op | source)
XLA Modules:
  0.0 27.7 jit_solution(9889241748875860671)
XLA Ops:
  0.6 26.1 %sweeps.1.m4 = f32[4,400,128]{2,1,0:T(8,128)S(1)} custom-call(f32[25,16,128]{2,1,0:T(8,128)} %t_hbm.1, f32[25,16,128]{2,1,0:T(8,128)} %s_hbm.1, f32[25,16,128]{2,1,0:T(8,128)} %u_hbm.1, f32[25,16,128]{2,1,0:T(8,128)} %v_hbm.1, s32[16,128]{1,0:T(8,128)} %b_hbm.1), custom_call_target="tpu_custom_call" | custom-call | tf_op jit(solution)/shard_map/sweeps/pallas_call | solution.py:412
  26.8 0.9 %write_out.1 = (f32[25,16,128]{2,1,0:T(8,128)}, f32[25,16,128]{2,1,0:T(8,128)}, f32[25,16,128]{2,1,0:T(8,128)}, f32[25,16,128]{2,1,0:T(8,128)}) custom-call(f32[4,400,128]{2,1,0:T(8,128)S(1)} %sweeps.1.m4), custom_call_target="tpu_custom_call" | custom-call | tf_op jit(solution)/shard_map/write_out/pallas_call | solution.py:435
